TPU v7x, 32 devices: a whole 2x2x4 slice. The times are simulated.
32 devices in a mesh: slab: 2 (over x), brick: 16 (over z, y, core).
Axes of the slice: x: 2, y: 2, z: 4, core: 2. Of those that a mesh axis runs over, the one named last changes fastest.
Arguments:
- features: bfloat16 [64, 64, 512], P(('slab', 'brick')), may hold values from -6 to 6
- weight: bfloat16 [27, 64, 64], replicated, may hold values from -0.15625 to 0.15625
- cotangent: bfloat16 [64, 64, 512], P(('slab', 'brick')), may hold values from -6 to 6
- occupancy: int32 [64, 24], P(('slab', 'brick')), may hold values from 0 to 4194303, as said below
- neighbours: int32 [64, 27], P(('slab', 'brick')), may hold values from -1 to 63, as said below
Outputs:
- output: bfloat16 [64, 64, 512], P(('slab', 'brick'))
- grad_input: bfloat16 [64, 64, 512], P(('slab', 'brick'))
- grad_weight: float32 [27, 64, 64], replicated
Inputs may be any that keep to these rules, and one draw needn't show every extreme that they name: `neighbours`: slot j of the device at (slab s, brick t), that is slot (16 s + t) * 2 + j, holds the brick of z layer 2 s + j and column t along x, at some row y; slot 0 of every device holds a brick, the others may be absent. For offset k = 9 (a + 1) + 3 (c + 1) + (e + 1), the entry of a present slot is the slot that holds the brick at layer 2 s + j + a, row y + c, column t + e if that brick is present, else -1; an absent slot's entries are all -1. The lists are symmetric, and the middle entry of a present slot is the slot itself. Bit j of word w of a slot is the occupancy of voxel 22 w + j; bits from voxel 512 on are zero. Absent slots are wholly unoccupied; slot 0 is fully occupied.
All inputs are finite; a program needn't handle non-finite values.
Results may differ from a plain program's by a relative error of at most 0.001.
Values may be sent and summed in bfloat16 or wider, within the bound.
A program may use at most 64 MiB of HBM per device.

v0:
```python
import math
import jax
import jax.numpy as jnp
from jax import lax
from jax.sharding import PartitionSpec as P

EDGE = 8


def extended(block, sides, width):
    for axis, dim in sides:
        count = lax.axis_size(axis)
        forward = [(i, i + 1) for i in range(count - 1)]
        backward = [(target, source) for source, target in forward]
        low = lax.ppermute(
            lax.slice_in_dim(block, block.shape[dim] - width, None, axis=dim), axis, forward
        )
        high = lax.ppermute(lax.slice_in_dim(block, 0, width, axis=dim), axis, backward)
        block = jnp.concatenate([low, block, high], axis=dim)
    return block


def unpack_bits(packed, voxels):
    places = jnp.arange(22, dtype=jnp.int32)
    bit_table = jnp.bitwise_and(jnp.right_shift(packed[..., :, None], places), 1)
    return bit_table.reshape(packed.shape[:-1] + (packed.shape[-1] * 22,))[..., :voxels]


def cut(length, side):
    if side < 0:
        return slice(length - 1, length)
    if side > 0:
        return slice(0, 1)
    return slice(0, length)


def windows(padded, direction):
    channels = padded.shape[0]
    pieces = []
    for shift_z in (-1, 0, 1):
        for shift_y in (-1, 0, 1):
            for shift_x in (-1, 0, 1):
                begin_z = 1 + direction * shift_z
                begin_y = 1 + direction * shift_y
                begin_x = 1 + direction * shift_x
                window = padded[
                    :, begin_z : begin_z + EDGE, begin_y : begin_y + EDGE, begin_x : begin_x + EDGE
                ]
                pieces.append(window.reshape(channels, EDGE * EDGE * EDGE))
    return jnp.stack(pieces, 0).reshape(27 * channels, EDGE * EDGE * EDGE)


def first_row(face):
    return face.reshape(face.shape[0], EDGE, EDGE)[:, 0, :]


def last_row(face):
    return face.reshape(face.shape[0], EDGE, EDGE)[:, EDGE - 1, :]


def per_device(features, weight, cotangent, occupancy, neighbours):
    slots = features.shape[0]
    channels = features.shape[1]
    voxels = features.shape[2]
    width = 2 * channels
    face_size = EDGE * EDGE
    occupied = unpack_bits(occupancy, voxels).astype(jnp.bfloat16)
    masked_input = features * occupied[:, None, :]
    masked_grad = cotangent * occupied[:, None, :]
    cube = jnp.concatenate([masked_input, masked_grad], 1).reshape(slots, width, EDGE, EDGE, EDGE)
    present = (neighbours >= 0).astype(jnp.bfloat16)
    low_x = cube[..., 0].reshape(slots, width, face_size)
    high_x = cube[..., EDGE - 1].reshape(slots, width, face_size)
    low_z = cube[0, :, 0].reshape(width, face_size)
    high_z = cube[slots - 1, :, EDGE - 1].reshape(width, face_size)
    payload = jnp.concatenate([low_x, high_x, low_z[None], high_z[None]], 0)
    beside_all = extended(payload[None, None], (("slab", 0), ("brick", 1)), 1)
    right_faces = beside_all[1, 2, :slots]
    left_faces = beside_all[1, 0, slots : 2 * slots]
    above_face = beside_all[2, 1, 2 * slots]
    below_face = beside_all[0, 1, 2 * slots + 1]
    above_right = first_row(beside_all[2, 2, 0])
    above_left = first_row(beside_all[2, 0, slots])
    below_right = last_row(beside_all[0, 2, slots - 1])
    below_left = last_row(beside_all[0, 0, 2 * slots - 1])

    def piece(slot, shift_z, shift_y, shift_x):
        target = slot + shift_z
        offset = 9 * (shift_z + 1) + 3 * (shift_y + 1) + (shift_x + 1)
        span_z = cut(EDGE, shift_z)
        span_y = cut(EDGE, shift_y)
        if 0 <= target < slots:
            if shift_x == 0:
                block = cube[target][:, span_z, span_y, :]
            else:
                source = right_faces if shift_x == 1 else left_faces
                block = source[target].reshape(width, EDGE, EDGE)[:, span_z, span_y][..., None]
        elif target >= slots:
            if shift_x == 0:
                block = above_face.reshape(width, EDGE, EDGE)[:, None, span_y, :]
            else:
                edge_row = above_right if shift_x == 1 else above_left
                block = edge_row[:, None, span_y, None]
        elif shift_x == 0:
            block = below_face.reshape(width, EDGE, EDGE)[:, None, span_y, :]
        else:
            edge_row = below_right if shift_x == 1 else below_left
            block = edge_row[:, None, span_y, None]
        return block * present[slot, offset]

    forward_matrix = jnp.transpose(weight, (1, 0, 2)).reshape(channels, 27 * channels)
    backward_matrix = jnp.transpose(weight, (2, 0, 1)).reshape(channels, 27 * channels)
    outputs = []
    gradients = []
    local_terms = jnp.zeros((channels, 27 * channels), jnp.float32)
    for slot in range(slots):
        layers = []
        for shift_z in (-1, 0, 1):
            rows = []
            for shift_y in (-1, 0, 1):
                columns = [piece(slot, shift_z, shift_y, shift_x) for shift_x in (-1, 0, 1)]
                rows.append(jnp.concatenate(columns, 3))
            layers.append(jnp.concatenate(rows, 2))
        padded = jnp.concatenate(layers, 1)
        scaling = occupied[slot].astype(jnp.float32)[None, :]
        input_patches = windows(padded[:channels], 1)
        output_rows = jnp.dot(forward_matrix, input_patches, preferred_element_type=jnp.float32)
        outputs.append((output_rows * scaling).astype(jnp.bfloat16))
        local_terms = local_terms + lax.dot_general(
            masked_grad[slot],
            input_patches,
            (((1,), (1,)), ((), ())),
            preferred_element_type=jnp.float32,
        )
        grad_patches = windows(padded[channels:], -1)
        grad_rows = jnp.dot(backward_matrix, grad_patches, preferred_element_type=jnp.float32)
        gradients.append((grad_rows * scaling).astype(jnp.bfloat16))
    total = lax.psum(local_terms, ("slab", "brick"))
    slot_count = slots * lax.axis_size("slab") * lax.axis_size("brick")
    grad_weight = jnp.transpose(total.reshape(channels, 27, channels), (1, 0, 2)) / math.sqrt(
        voxels * slot_count
    )
    return (jnp.stack(outputs, 0), jnp.stack(gradients, 0), grad_weight)


def solution(mesh):
    placed = (
        P(("slab", "brick"), None, None),
        P(),
        P(("slab", "brick"), None, None),
        P(("slab", "brick"), None),
        P(("slab", "brick"), None),
    )
    return jax.shard_map(
        per_device,
        mesh=mesh,
        in_specs=placed,
        out_specs=(P(("slab", "brick"), None, None), P(("slab", "brick"), None, None), P()),
        check_vma=False,
    )
```

profile of v0, /device:TPU:1, one launch (start us, length us, event | category | flops | bytes accessed | tf_op | source)
XLA Modules:
  0.0 351.3 jit_solution(4987366351810817979)
XLA Ops:
  12.2 4.0 %collective-permute-start = (bf16[1,1,6,128,64]{3,4,2,1,0:T(8,128)(2,1)S(1)}, bf16[1,1,6,128,64]{3,4,2,1,0:T(8,128)(2,1)S(1)}, u32[]{:S(2)}, u32[]{:S(2)}) collective-permute-start(bf16[1,1,6,128,64]{3,4,2,1,0:T(8,128)(2,1)S(1)} %maximum_bitcast_fusion), channel_id=1, source_target_pairs={{0,16},{1,17},{2,18},{3,19},{4,20},{5,21},{6,22},{7,23},{8,24},{9,... | collective-permute-start | bytes 294920 | tf_op jit(solution)/shard_map/ppermute | solution.py:15
  22.9 1.9 slice_multiply_fusion.19
  27.4 1.8 slice_multiply_fusion.15
  29.3 2.8 collective-permute-start.3
  32.1 4.2 %collective-permute-start.2 = (bf16[3,1,6,128,64]{3,4,2,1,0:T(8,128)(2,1)S(1)}, bf16[3,1,6,128,64]{3,4,2,1,0:T(8,128)(2,1)S(1)}, u32[]{:S(2)}, u32[]{:S(2)}) collective-permute-start(bf16[3,1,6,128,64]{3,4,2,1,0:T(8,128)(2,1)S(1)} %pad_maximum_fusion), channel_id=1, source_target_pairs={{0,1},{1,2},{2,3},{3,4},{4,5},{5,6},{6,7},{7,8},{8,9},{9,10},{10,1... | collective-permute-start | bytes 884744 | tf_op jit(solution)/shard_map/ppermute | solution.py:15
  38.7 1.8 fusion.28
  40.5 1.9 fusion.34
  69.4 1.6 copy.308
  71.0 1.6 copy.307
  72.7 1.6 copy.306
  74.3 1.6 copy.259
  111.3 2.0 fusion.45
  113.3 2.0 fusion.46
  120.4 1.6 copy.275
  123.6 1.6 copy.273
  128.5 1.6 copy.270
  133.3 1.6 copy.228
  134.9 1.7 copy.227
  154.0 2.1 fusion.41
  156.1 1.9 fusion.42
  159.8 1.6 copy.323
  161.4 1.6 copy.322
  176.8 1.6 fusion.50
  181.6 1.6 copy.303
  186.5 1.6 copy.300
  188.1 1.6 copy.299
  189.7 1.6 copy.298
  191.4 1.6 copy.297
  194.6 1.6 copy.267
  196.2 1.6 copy.266
  199.5 1.6 copy.264
  219.3 122.2 %all-reduce.2.cloned.1.call-done = f32[64,1728]{1,0:T(8,128)} async-done(((f32[64,1728]{1,0:T(8,128)}), f32[64,1728]{1,0:T(8,128)}) %all-reduce.2.cloned.1.call-update) | async-done | bytes 442384 | tf_op jit(solution)/shard_map/psum | solution.py:138
  (575 shorter events, 153.3 us)
Async XLA Ops:
  7.2 143.5 %copy-start = (bf16[27,64,64]{2,1,0:T(8,128)(2,1)S(1)}, bf16[27,64,64]{2,1,0:T(8,128)(2,1)}, u32[]{:S(2)}) copy-start(bf16[27,64,64]{2,1,0:T(8,128)(2,1)} %param.6) | copy-start | bytes 663556
  7.2 334.3 %all-reduce.2.cloned.1.call-start = ((), (), s32[]{:S(2)}) async-start(), calls=%async_computation | async-start | bytes 917504 | tf_op jit(solution)/shard_map/psum | solution.py:138
  10.9 18.3 %collective-permute-start.1 = (bf16[1,1,6,128,64]{3,4,2,1,0:T(8,128)(2,1)S(1)}, bf16[1,1,6,128,64]{3,4,2,1,0:T(8,128)(2,1)S(1)}, u32[]{:S(2)}, u32[]{:S(2)}) collective-permute-start(bf16[1,1,6,128,64]{3,4,2,1,0:T(8,128)(2,1)S(1)} %maximum_bitcast_fusion), channel_id=1, source_target_pairs={{16,0},{17,1},{18,2},{19,3},{20,4},{21,5},{22,6},{23,7},{24,8},{25... | collective-permute-start | bytes 294920 | tf_op jit(solution)/shard_map/ppermute | solution.py:18
  12.2 17.0 %collective-permute-start = (bf16[1,1,6,128,64]{3,4,2,1,0:T(8,128)(2,1)S(1)}, bf16[1,1,6,128,64]{3,4,2,1,0:T(8,128)(2,1)S(1)}, u32[]{:S(2)}, u32[]{:S(2)}) collective-permute-start(bf16[1,1,6,128,64]{3,4,2,1,0:T(8,128)(2,1)S(1)} %maximum_bitcast_fusion), channel_id=1, source_target_pairs={{0,16},{1,17},{2,18},{3,19},{4,20},{5,21},{6,22},{7,23},{8,24},{9,... | collective-permute-start | bytes 294920 | tf_op jit(solution)/shard_map/ppermute | solution.py:15
  27.4 33.3 %copy-start.86 = (bf16[128,8,1,8]{0,3,2,1:T(8,128)(2,1)}, bf16[128,8,1,8]{0,3,2,1:T(8,128)(2,1)S(1)}, u32[]{:S(2)}) copy-start(bf16[128,8,1,8]{0,3,2,1:T(8,128)(2,1)S(1)} %get-tuple-element.145) | copy-start | bytes 49156
  27.4 33.3 %copy-start.88 = (bf16[128,8,1,8]{0,3,2,1:T(8,128)(2,1)}, bf16[128,8,1,8]{0,3,2,1:T(8,128)(2,1)S(1)}, u32[]{:S(2)}) copy-start(bf16[128,8,1,8]{0,3,2,1:T(8,128)(2,1)S(1)} %get-tuple-element.146) | copy-start | bytes 49156
  29.3 13.1 %collective-permute-start.3 = (bf16[3,1,6,128,64]{3,4,2,1,0:T(8,128)(2,1)S(1)}, bf16[3,1,6,128,64]{3,4,2,1,0:T(8,128)(2,1)S(1)}, u32[]{:S(2)}, u32[]{:S(2)}) collective-permute-start(bf16[3,1,6,128,64]{3,4,2,1,0:T(8,128)(2,1)S(1)} %pad_maximum_fusion), channel_id=1, source_target_pairs={{1,0},{2,1},{3,2},{4,3},{5,4},{6,5},{7,6},{8,7},{9,8},{10,9},{11,1... | collective-permute-start | bytes 884744 | tf_op jit(solution)/shard_map/ppermute | solution.py:18
  32.1 18.9 %collective-permute-start.2 = (bf16[3,1,6,128,64]{3,4,2,1,0:T(8,128)(2,1)S(1)}, bf16[3,1,6,128,64]{3,4,2,1,0:T(8,128)(2,1)S(1)}, u32[]{:S(2)}, u32[]{:S(2)}) collective-permute-start(bf16[3,1,6,128,64]{3,4,2,1,0:T(8,128)(2,1)S(1)} %pad_maximum_fusion), channel_id=1, source_target_pairs={{0,1},{1,2},{2,3},{3,4},{4,5},{5,6},{6,7},{7,8},{8,9},{9,10},{10,1... | collective-permute-start | bytes 884744 | tf_op jit(solution)/shard_map/ppermute | solution.py:15
  43.6 21.7 %copy-start.116 = (bf16[128,8,8]{0,2,1:T(8,128)(2,1)}, bf16[128,8,8]{0,2,1:T(8,128)(2,1)S(1)}, u32[]{:S(2)}) copy-start(bf16[128,8,8]{0,2,1:T(8,128)(2,1)S(1)} %get-tuple-element.117) | copy-start | bytes 49156
  47.3 13.4 %copy-start.102 = (bf16[128,8,1,1]{0,3,2,1:T(2,128)(2,1)}, bf16[128,8,1,1]{0,3,2,1:T(2,128)(2,1)S(1)}, u32[]{:S(2)}) copy-start(bf16[128,8,1,1]{0,3,2,1:T(2,128)(2,1)S(1)} %copy.198) | copy-start | bytes 6148
  47.3 13.4 %copy-start.104 = (bf16[128,8,1,1]{0,3,2,1:T(2,128)(2,1)}, bf16[128,8,1,1]{0,3,2,1:T(2,128)(2,1)S(1)}, u32[]{:S(2)}) copy-start(bf16[128,8,1,1]{0,3,2,1:T(2,128)(2,1)S(1)} %copy.192) | copy-start | bytes 6148
  52.4 14.2 %copy-start.117 = (bf16[128,8,8]{0,2,1:T(8,128)(2,1)}, bf16[128,8,8]{0,2,1:T(8,128)(2,1)S(1)}, u32[]{:S(2)}) copy-start(bf16[128,8,8]{0,2,1:T(8,128)(2,1)S(1)} %get-tuple-element.111) | copy-start | bytes 49156
  99.5 15.7 %copy-start.113 = (bf16[128,1,8,8]{0,3,2,1:T(8,128)(2,1)S(1)}, bf16[128,1,8,8]{0,3,2,1:T(8,128)(2,1)}, u32[]{:S(2)}) copy-start(bf16[128,1,8,8]{0,3,2,1:T(8,128)(2,1)} %slice_multiply_fusion.3) | copy-start | bytes 49156
  99.5 15.7 %copy-start.122 = (bf16[128,1,8,1]{0,3,2,1:T(2,128)(2,1)S(1)}, bf16[128,1,8,1]{0,3,2,1:T(2,128)(2,1)}, u32[]{:S(2)}) copy-start(bf16[128,1,8,1]{0,3,2,1:T(2,128)(2,1)} %copy.202) | copy-start | bytes 6148
  99.5 15.7 %copy-start.123 = (bf16[128,1,8,1]{0,3,2,1:T(2,128)(2,1)S(1)}, bf16[128,1,8,1]{0,3,2,1:T(2,128)(2,1)}, u32[]{:S(2)}) copy-start(bf16[128,1,8,1]{0,3,2,1:T(2,128)(2,1)} %copy.201) | copy-start | bytes 6148
  99.6 15.7 %copy-start.130 = (bf16[128,1,1,8]{0,3,2,1:T(8,128)(2,1)S(1)}, bf16[128,1,1,8]{0,3,2,1:T(8,128)(2,1)}, u32[]{:S(2)}) copy-start(bf16[128,1,1,8]{0,3,2,1:T(8,128)(2,1)} %get-tuple-element.143) | copy-start | bytes 6148
  99.6 15.8 %copy-start.131 = (bf16[128,1,1,8]{0,3,2,1:T(8,128)(2,1)S(1)}, bf16[128,1,1,8]{0,3,2,1:T(8,128)(2,1)}, u32[]{:S(2)}) copy-start(bf16[128,1,1,8]{0,3,2,1:T(8,128)(2,1)} %get-tuple-element.144) | copy-start | bytes 6148
  134.9 14.7 %copy-start.20 = (bf16[1,64,512]{2,1,0:T(8,128)(2,1)S(1)}, bf16[1,64,512]{2,1,0:T(8,128)(2,1)}, u32[]{:S(2)}) copy-start(bf16[1,64,512]{2,1,0:T(8,128)(2,1)} %copy.220) | copy-start | bytes 196612
  137.3 12.2 %copy-start.24 = (bf16[1,64,512]{2,1,0:T(8,128)(2,1)S(1)}, bf16[1,64,512]{2,1,0:T(8,128)(2,1)}, u32[]{:S(2)}) copy-start(bf16[1,64,512]{2,1,0:T(8,128)(2,1)} %copy.218) | copy-start | bytes 196612
  137.3 12.3 %copy-start.23 = (bf16[1,64,512]{2,1,0:T(8,128)(2,1)S(1)}, bf16[1,64,512]{2,1,0:T(8,128)(2,1)}, u32[]{:S(2)}) copy-start(bf16[1,64,512]{2,1,0:T(8,128)(2,1)} %copy.219) | copy-start | bytes 196612
  138.0 11.4 %copy-start.42 = (bf16[1,64,512]{2,1,0:T(8,128)(2,1)S(1)}, bf16[1,64,512]{2,1,0:T(8,128)(2,1)}, u32[]{:S(2)}) copy-start(bf16[1,64,512]{2,1,0:T(8,128)(2,1)} %copy.215) | copy-start | bytes 196612
  138.0 11.5 %copy-start.39 = (bf16[1,64,512]{2,1,0:T(8,128)(2,1)S(1)}, bf16[1,64,512]{2,1,0:T(8,128)(2,1)}, u32[]{:S(2)}) copy-start(bf16[1,64,512]{2,1,0:T(8,128)(2,1)} %copy.217) | copy-start | bytes 196612
  161.4 12.7 %copy-start.134 = (bf16[128,8]{0,1:T(8,128)(2,1)S(1)}, bf16[128,8]{0,1:T(8,128)(2,1)}, u32[]{:S(2)}) copy-start(bf16[128,8]{0,1:T(8,128)(2,1)} %get-tuple-element.174) | copy-start | bytes 6148
  161.4 13.9 %copy-start.135 = (bf16[128,8]{0,1:T(8,128)(2,1)S(1)}, bf16[128,8]{0,1:T(8,128)(2,1)}, u32[]{:S(2)}) copy-start(bf16[128,8]{0,1:T(8,128)(2,1)} %get-tuple-element.172) | copy-start | bytes 6148
  161.4 15.1 %copy-start.110 = (bf16[128,1,8,8]{0,3,2,1:T(8,128)(2,1)S(1)}, bf16[128,1,8,8]{0,3,2,1:T(8,128)(2,1)}, u32[]{:S(2)}) copy-start(bf16[128,1,8,8]{0,3,2,1:T(8,128)(2,1)} %get-tuple-element.153) | copy-start | bytes 49156
  161.4 15.1 %copy-start.118 = (bf16[128,1,8,1]{0,3,2,1:T(2,128)(2,1)S(1)}, bf16[128,1,8,1]{0,3,2,1:T(2,128)(2,1)}, u32[]{:S(2)}) copy-start(bf16[128,1,8,1]{0,3,2,1:T(2,128)(2,1)} %copy.241) | copy-start | bytes 6148
  161.4 15.1 %copy-start.119 = (bf16[128,1,8,1]{0,3,2,1:T(2,128)(2,1)S(1)}, bf16[128,1,8,1]{0,3,2,1:T(2,128)(2,1)}, u32[]{:S(2)}) copy-start(bf16[128,1,8,1]{0,3,2,1:T(2,128)(2,1)} %copy.240) | copy-start | bytes 6148
  161.4 15.1 %copy-start.126 = (bf16[128,1,1,8]{0,3,2,1:T(8,128)(2,1)S(1)}, bf16[128,1,1,8]{0,3,2,1:T(8,128)(2,1)}, u32[]{:S(2)}) copy-start(bf16[128,1,1,8]{0,3,2,1:T(8,128)(2,1)} %get-tuple-element.169) | copy-start | bytes 6148
  161.4 15.1 %copy-start.127 = (bf16[128,1,1,8]{0,3,2,1:T(8,128)(2,1)S(1)}, bf16[128,1,1,8]{0,3,2,1:T(8,128)(2,1)}, u32[]{:S(2)}) copy-start(bf16[128,1,1,8]{0,3,2,1:T(8,128)(2,1)} %get-tuple-element.170) | copy-start | bytes 6148
  196.2 17.3 %copy-start.10 = (bf16[1,64,512]{2,1,0:T(8,128)(2,1)S(1)}, bf16[1,64,512]{2,1,0:T(8,128)(2,1)}, u32[]{:S(2)}) copy-start(bf16[1,64,512]{2,1,0:T(8,128)(2,1)} %copy.259) | copy-start | bytes 196612
  201.8 11.7 %copy-start.12 = (bf16[1,64,512]{2,1,0:T(8,128)(2,1)S(1)}, bf16[1,64,512]{2,1,0:T(8,128)(2,1)}, u32[]{:S(2)}) copy-start(bf16[1,64,512]{2,1,0:T(8,128)(2,1)} %copy.257) | copy-start | bytes 196612
  201.8 11.7 %copy-start.11 = (bf16[1,64,512]{2,1,0:T(8,128)(2,1)S(1)}, bf16[1,64,512]{2,1,0:T(8,128)(2,1)}, u32[]{:S(2)}) copy-start(bf16[1,64,512]{2,1,0:T(8,128)(2,1)} %copy.258) | copy-start | bytes 196612
  (112 other events, 509.4 us)
Sparse Core Ops, SparseCore 0:
  215.4 126.0 all-reduce.1
where the time goes:
time: 354 us; the launch traced here: 351 us
  local copies, waits for them, and re-layouts  145 us (41%)
  waiting for transfers between devices  122 us (34%)
  other arithmetic  49.6 us (14%)
  between operations  16.8 us (5%)
  starting transfers between devices  12.3 us (3%)
  matrix products  5.18 us (1%)
    psum x1, waiting for transfers between devices, per_device(): total = lax.psum(local_terms, ('slab', 'brick'))  122 us
    another operation x112, local copies, waits for them, and re-layouts, windows(): return jnp.stack(pieces, 0).reshape(27 * channels, EDGE * EDGE * EDGE)  106 us
    mul x34, other arithmetic, piece(): return block * present[slot, offset]  41.1 us
    unnamed x386, local copies, waits for them, and re-layouts  24 us
    ppermute x2, starting transfers between devices, extended(): lax.ppermute(lax.slice_in_dim(block, block.shape[dim] - width, None, axis...  8.19 us
  transfers between devices with their start and end apart: 5, of which 1 were waited for; matrix products, arithmetic and copies ran while one was open for 9% of the time, Pallas kernels for 0%

commit v1 on v0

--- a/solution.py
+++ b/solution.py
@@ -135,7 +135,7 @@
         grad_patches = windows(padded[channels:], -1)
         grad_rows = jnp.dot(backward_matrix, grad_patches, preferred_element_type=jnp.float32)
         gradients.append((grad_rows * scaling).astype(jnp.bfloat16))
-    total = lax.psum(local_terms, ("slab", "brick"))
+    total = jnp.sum(lax.all_gather(local_terms, ("slab", "brick")), axis=0)
     slot_count = slots * lax.axis_size("slab") * lax.axis_size("brick")
     grad_weight = jnp.transpose(total.reshape(channels, 27, channels), (1, 0, 2)) / math.sqrt(
         voxels * slot_count

time: 354 us -> 282 us (0.80)
  waiting for transfers between devices: 122 us -> 21.4 us
  local copies, waits for them, and re-layouts: 145 us -> 167 us
  other arithmetic: 49.6 us -> 56.7 us
    psum x1 -> x0, waiting for transfers between devices: 122 us -> none  [per_device(): total = lax.psum(local_terms, ('slab', 'brick'))]
    all_gather x0 -> x1, waiting for transfers between devices: none -> 21.1 us  [per_device(): total = jnp.sum(lax.all_gather(local_terms, ('slab', 'brick')), axis=0)]
    unnamed x386 -> x362, local copies, waits for them, and re-layouts: 24 us -> 35.7 us
    another operation x112, local copies, waits for them, and re-layouts: 106 us -> 116 us  [windows(): return jnp.stack(pieces, 0).reshape(27 * channels, EDGE * EDGE * EDGE)]
    reduce_sum x0 -> x1, other arithmetic: none -> 5.91 us  [per_device(): total = jnp.sum(lax.all_gather(local_terms, ('slab', 'brick')), axis=0)]
    mul x16, local copies, waits for them, and re-layouts: 4.88 us -> 0.18 us  [piece(): return block * present[slot, offset]]
  transfers between devices with their start and end apart: 5 -> 5, of which waited for: 1 -> 1; matrix products, arithmetic and copies ran while one was open for 9% -> 36% of each run, Pallas kernels for 0% -> 0%
where the time goes in v1:
time: 282 us; the launch traced here: 278 us
  local copies, waits for them, and re-layouts  167 us (59%)
  other arithmetic  56.7 us (20%)
  waiting for transfers between devices  21.4 us (8%)
  between operations  16.5 us (6%)
  starting transfers between devices  12.3 us (4%)
  matrix products  3.91 us (1%)
    another operation x112, local copies, waits for them, and re-layouts, windows(): return jnp.stack(pieces, 0).reshape(27 * channels, EDGE * EDGE * EDGE)  116 us
    mul x34, other arithmetic, piece(): return block * present[slot, offset]  40.6 us
    unnamed x362, local copies, waits for them, and re-layouts  35.7 us
    all_gather x1, waiting for transfers between devices, per_device(): total = jnp.sum(lax.all_gather(local_terms, ('slab', 'brick')), axis=0)  21.1 us
    slice x8, local copies, waits for them, and re-layouts, windows(): padded[:, begin_z:begin_z + EDGE, begin_y:begin_y + EDGE, begin_x:begin_x...  10.3 us
    ppermute x2, starting transfers between devices, extended(): lax.ppermute(lax.slice_in_dim(block, block.shape[dim] - width, None, axis...  8.19 us
    reduce_sum x1, other arithmetic, per_device(): total = jnp.sum(lax.all_gather(local_terms, ('slab', 'brick')), axis=0)  5.91 us
  transfers between devices with their start and end apart: 5, of which 1 were waited for; matrix products, arithmetic and copies ran while one was open for 36% of the time, Pallas kernels for 0%

profile of v1, /device:TPU:1, one launch (start us, length us, event | category | flops | bytes accessed | tf_op | source)
XLA Modules:
  0.0 278.0 jit_solution(2947074065611686275)
XLA Ops:
  12.8 4.0 %collective-permute-start = (bf16[1,1,6,128,64]{3,4,2,1,0:T(8,128)(2,1)S(1)}, bf16[1,1,6,128,64]{3,4,2,1,0:T(8,128)(2,1)S(1)}, u32[]{:S(2)}, u32[]{:S(2)}) collective-permute-start(bf16[1,1,6,128,64]{3,4,2,1,0:T(8,128)(2,1)S(1)} %maximum_bitcast_fusion), channel_id=1, source_target_pairs={{0,16},{1,17},{2,18},{3,19},{4,20},{5,21},{6,22},{7,23},{8,24},{9,... | collective-permute-start | bytes 294920 | tf_op jit(solution)/shard_map/ppermute | solution.py:15
  26.2 1.8 slice_multiply_fusion.19
  28.1 2.8 %collective-permute-start.3 = (bf16[3,1,6,128,64]{3,4,2,1,0:T(8,128)(2,1)S(1)}, bf16[3,1,6,128,64]{3,4,2,1,0:T(8,128)(2,1)S(1)}, u32[]{:S(2)}, u32[]{:S(2)}) collective-permute-start(bf16[3,1,6,128,64]{3,4,2,1,0:T(8,128)(2,1)S(1)} %pad_maximum_fusion), channel_id=1, source_target_pairs={{1,0},{2,1},{3,2},{4,3},{5,4},{6,5},{7,6},{8,7},{9,8},{10,9},{11,1... | collective-permute-start | bytes 884744 | tf_op jit(solution)/shard_map/ppermute | solution.py:18
  30.9 4.2 %collective-permute-start.2 = (bf16[3,1,6,128,64]{3,4,2,1,0:T(8,128)(2,1)S(1)}, bf16[3,1,6,128,64]{3,4,2,1,0:T(8,128)(2,1)S(1)}, u32[]{:S(2)}, u32[]{:S(2)}) collective-permute-start(bf16[3,1,6,128,64]{3,4,2,1,0:T(8,128)(2,1)S(1)} %pad_maximum_fusion), channel_id=1, source_target_pairs={{0,1},{1,2},{2,3},{3,4},{4,5},{5,6},{6,7},{7,8},{8,9},{9,10},{10,1... | collective-permute-start | bytes 884744 | tf_op jit(solution)/shard_map/ppermute | solution.py:15
  37.6 1.9 fusion.28
  39.5 1.9 fusion.34
  41.4 1.9 slice_bitcast_fusion.6
  43.3 1.9 slice_bitcast_fusion.7
  59.4 1.6 copy.243
  96.8 1.8 fusion.47
  101.8 1.6 copy.204
  108.2 1.6 copy.208
  114.2 1.6 copy.211
  124.8 1.6 copy.217
  130.6 2.0 fusion.45
  132.6 1.9 fusion.46
  162.8 1.6 copy.301
  164.5 1.6 copy.302
  166.9 1.7 copy.304
  171.8 1.6 copy.307
  191.1 1.6 copy.270
  192.7 1.7 copy.271
  194.4 1.7 copy.272
  196.1 1.7 copy.273
  197.7 1.7 copy.274
  199.4 1.7 copy.275
  201.0 1.7 copy.276
  202.7 1.6 copy.277
  209.7 1.6 copy.283
  211.3 1.6 copy.284
  242.2 21.1 %all-gather.3.cloned.1.call-done = f32[2048,1728]{1,0:T(8,128)} async-done(((f32[64,1728]{1,0:T(8,128)}), f32[2048,1728]{1,0:T(8,128)}) %all-gather.3.cloned.1.call-update) | async-done | bytes 14155792 | tf_op jit(solution)/shard_map/all_gather | solution.py:138
  263.3 5.9 %reduce_sum.9 = f32[64,1728]{1,0:T(8,128)S(1)} reduce(f32[32,64,1728]{2,1,0:T(8,128)} %bitcast.363, f32[]{:T(128)} %constant.3.clone.1), dimensions={0}, to_apply=%region_0.0 | reduce | flops 3428352 | bytes 14598148 | tf_op jit(solution)/shard_map/reduce_sum | solution.py:138
  (552 shorter events, 177.1 us)
Async XLA Ops:
  7.2 230.9 %copy-start = (bf16[27,64,64]{2,1,0:T(8,128)(2,1)S(1)}, bf16[27,64,64]{2,1,0:T(8,128)(2,1)}, u32[]{:S(2)}) copy-start(bf16[27,64,64]{2,1,0:T(8,128)(2,1)} %param.6) | copy-start | bytes 663556
  7.2 256.2 %all-gather.3.cloned.1.call-start = ((), (), s32[]{:S(2)}) async-start(), calls=%async_computation | async-start | bytes 15138816 | tf_op jit(solution)/shard_map/all_gather | solution.py:138
  11.5 16.5 %collective-permute-start.1 = (bf16[1,1,6,128,64]{3,4,2,1,0:T(8,128)(2,1)S(1)}, bf16[1,1,6,128,64]{3,4,2,1,0:T(8,128)(2,1)S(1)}, u32[]{:S(2)}, u32[]{:S(2)}) collective-permute-start(bf16[1,1,6,128,64]{3,4,2,1,0:T(8,128)(2,1)S(1)} %maximum_bitcast_fusion), channel_id=1, source_target_pairs={{16,0},{17,1},{18,2},{19,3},{20,4},{21,5},{22,6},{23,7},{24,8},{25... | collective-permute-start | bytes 294920 | tf_op jit(solution)/shard_map/ppermute | solution.py:18
  12.8 15.2 %collective-permute-start = (bf16[1,1,6,128,64]{3,4,2,1,0:T(8,128)(2,1)S(1)}, bf16[1,1,6,128,64]{3,4,2,1,0:T(8,128)(2,1)S(1)}, u32[]{:S(2)}, u32[]{:S(2)}) collective-permute-start(bf16[1,1,6,128,64]{3,4,2,1,0:T(8,128)(2,1)S(1)} %maximum_bitcast_fusion), channel_id=1, source_target_pairs={{0,16},{1,17},{2,18},{3,19},{4,20},{5,21},{6,22},{7,23},{8,24},{9,... | collective-permute-start | bytes 294920 | tf_op jit(solution)/shard_map/ppermute | solution.py:15
  23.6 30.6 %copy-start.95 = (bf16[128,8,1,8]{0,3,2,1:T(8,128)(2,1)}, bf16[128,8,1,8]{0,3,2,1:T(8,128)(2,1)S(1)}, u32[]{:S(2)}) copy-start(bf16[128,8,1,8]{0,3,2,1:T(8,128)(2,1)S(1)} %get-tuple-element.150) | copy-start | bytes 49156
  28.1 13.3 %collective-permute-start.3 = (bf16[3,1,6,128,64]{3,4,2,1,0:T(8,128)(2,1)S(1)}, bf16[3,1,6,128,64]{3,4,2,1,0:T(8,128)(2,1)S(1)}, u32[]{:S(2)}, u32[]{:S(2)}) collective-permute-start(bf16[3,1,6,128,64]{3,4,2,1,0:T(8,128)(2,1)S(1)} %pad_maximum_fusion), channel_id=1, source_target_pairs={{1,0},{2,1},{3,2},{4,3},{5,4},{6,5},{7,6},{8,7},{9,8},{10,9},{11,1... | collective-permute-start | bytes 884744 | tf_op jit(solution)/shard_map/ppermute | solution.py:18
  30.9 12.4 %collective-permute-start.2 = (bf16[3,1,6,128,64]{3,4,2,1,0:T(8,128)(2,1)S(1)}, bf16[3,1,6,128,64]{3,4,2,1,0:T(8,128)(2,1)S(1)}, u32[]{:S(2)}, u32[]{:S(2)}) collective-permute-start(bf16[3,1,6,128,64]{3,4,2,1,0:T(8,128)(2,1)S(1)} %pad_maximum_fusion), channel_id=1, source_target_pairs={{0,1},{1,2},{2,3},{3,4},{4,5},{5,6},{6,7},{7,8},{8,9},{9,10},{10,1... | collective-permute-start | bytes 884744 | tf_op jit(solution)/shard_map/ppermute | solution.py:15
  114.2 20.4 %copy-start.102 = (bf16[128,8,1,1]{0,3,2,1:T(2,128)(2,1)S(1)}, bf16[128,8,1,1]{0,3,2,1:T(2,128)(2,1)}, u32[]{:S(2)}) copy-start(bf16[128,8,1,1]{0,3,2,1:T(2,128)(2,1)} %copy-done.101) | copy-start | bytes 6148
  114.2 20.4 %copy-start.104 = (bf16[128,8,1,1]{0,3,2,1:T(2,128)(2,1)S(1)}, bf16[128,8,1,1]{0,3,2,1:T(2,128)(2,1)}, u32[]{:S(2)}) copy-start(bf16[128,8,1,1]{0,3,2,1:T(2,128)(2,1)} %copy-done.103) | copy-start | bytes 6148
  114.2 20.4 %copy-start.106 = (bf16[128,8,1,1]{0,3,2,1:T(2,128)(2,1)S(1)}, bf16[128,8,1,1]{0,3,2,1:T(2,128)(2,1)}, u32[]{:S(2)}) copy-start(bf16[128,8,1,1]{0,3,2,1:T(2,128)(2,1)} %copy-done.105) | copy-start | bytes 6148
  114.2 20.4 %copy-start.108 = (bf16[128,8,1,1]{0,3,2,1:T(2,128)(2,1)S(1)}, bf16[128,8,1,1]{0,3,2,1:T(2,128)(2,1)}, u32[]{:S(2)}) copy-start(bf16[128,8,1,1]{0,3,2,1:T(2,128)(2,1)} %copy-done.107) | copy-start | bytes 6148
  114.2 20.4 %copy-start.113 = (bf16[128,1,8,8]{0,3,2,1:T(8,128)(2,1)S(1)}, bf16[128,1,8,8]{0,3,2,1:T(8,128)(2,1)}, u32[]{:S(2)}) copy-start(bf16[128,1,8,8]{0,3,2,1:T(8,128)(2,1)} %slice_multiply_fusion.3) | copy-start | bytes 49156
  160.7 23.0 %copy-start.11 = (bf16[64,8,8,8]{0,3,2,1:T(8,128)(2,1)S(1)}, bf16[64,8,8,8]{0,3,2,1:T(8,128)(2,1)}, u32[]{:S(2)}) copy-start(bf16[64,8,8,8]{0,3,2,1:T(8,128)(2,1)} %get-tuple-element.53) | copy-start | bytes 196612
  161.4 23.0 %copy-start.10 = (bf16[64,8,8,8]{0,3,2,1:T(8,128)(2,1)S(1)}, bf16[64,8,8,8]{0,3,2,1:T(8,128)(2,1)}, u32[]{:S(2)}) copy-start(bf16[64,8,8,8]{0,3,2,1:T(8,128)(2,1)} %get-tuple-element.52) | copy-start | bytes 196612
  162.1 23.0 %copy-start.9 = (bf16[64,8,8,8]{0,3,2,1:T(8,128)(2,1)S(1)}, bf16[64,8,8,8]{0,3,2,1:T(8,128)(2,1)}, u32[]{:S(2)}) copy-start(bf16[64,8,8,8]{0,3,2,1:T(8,128)(2,1)} %get-tuple-element.51) | copy-start | bytes 196612
  162.8 23.0 %copy-start.8 = (bf16[64,8,8,8]{0,3,2,1:T(8,128)(2,1)S(1)}, bf16[64,8,8,8]{0,3,2,1:T(8,128)(2,1)}, u32[]{:S(2)}) copy-start(bf16[64,8,8,8]{0,3,2,1:T(8,128)(2,1)} %get-tuple-element.50) | copy-start | bytes 196612
  164.5 22.1 %copy-start.7 = (bf16[64,8,8,8]{0,3,2,1:T(8,128)(2,1)S(1)}, bf16[64,8,8,8]{0,3,2,1:T(8,128)(2,1)}, u32[]{:S(2)}) copy-start(bf16[64,8,8,8]{0,3,2,1:T(8,128)(2,1)} %get-tuple-element.49) | copy-start | bytes 196612
  166.1 21.2 %copy-start.6 = (bf16[64,8,8,8]{0,3,2,1:T(8,128)(2,1)S(1)}, bf16[64,8,8,8]{0,3,2,1:T(8,128)(2,1)}, u32[]{:S(2)}) copy-start(bf16[64,8,8,8]{0,3,2,1:T(8,128)(2,1)} %get-tuple-element.48) | copy-start | bytes 196612
  166.9 21.2 %copy-start.5 = (bf16[64,8,8,8]{0,3,2,1:T(8,128)(2,1)S(1)}, bf16[64,8,8,8]{0,3,2,1:T(8,128)(2,1)}, u32[]{:S(2)}) copy-start(bf16[64,8,8,8]{0,3,2,1:T(8,128)(2,1)} %get-tuple-element.47) | copy-start | bytes 196612
  184.4 23.2 %copy-start.19 = (bf16[64,8,8,8]{0,3,2,1:T(8,128)(2,1)S(1)}, bf16[64,8,8,8]{0,3,2,1:T(8,128)(2,1)}, u32[]{:S(2)}) copy-start(bf16[64,8,8,8]{0,3,2,1:T(8,128)(2,1)} %get-tuple-element.136) | copy-start | bytes 196612
  185.1 23.2 %copy-start.18 = (bf16[64,8,8,8]{0,3,2,1:T(8,128)(2,1)S(1)}, bf16[64,8,8,8]{0,3,2,1:T(8,128)(2,1)}, u32[]{:S(2)}) copy-start(bf16[64,8,8,8]{0,3,2,1:T(8,128)(2,1)} %get-tuple-element.137) | copy-start | bytes 196612
  185.8 23.2 %copy-start.17 = (bf16[64,8,8,8]{0,3,2,1:T(8,128)(2,1)S(1)}, bf16[64,8,8,8]{0,3,2,1:T(8,128)(2,1)}, u32[]{:S(2)}) copy-start(bf16[64,8,8,8]{0,3,2,1:T(8,128)(2,1)} %get-tuple-element.127) | copy-start | bytes 196612
  191.1 26.2 %copy-start.26 = (bf16[64,8,8,8]{0,3,2,1:T(8,128)(2,1)S(1)}, bf16[64,8,8,8]{0,3,2,1:T(8,128)(2,1)}, u32[]{:S(2)}) copy-start(bf16[64,8,8,8]{0,3,2,1:T(8,128)(2,1)} %get-tuple-element.17) | copy-start | bytes 196612
  192.7 24.6 %copy-start.25 = (bf16[64,8,8,8]{0,3,2,1:T(8,128)(2,1)S(1)}, bf16[64,8,8,8]{0,3,2,1:T(8,128)(2,1)}, u32[]{:S(2)}) copy-start(bf16[64,8,8,8]{0,3,2,1:T(8,128)(2,1)} %get-tuple-element.16) | copy-start | bytes 196612
  194.4 23.1 %copy-start.24 = (bf16[64,8,8,8]{0,3,2,1:T(8,128)(2,1)S(1)}, bf16[64,8,8,8]{0,3,2,1:T(8,128)(2,1)}, u32[]{:S(2)}) copy-start(bf16[64,8,8,8]{0,3,2,1:T(8,128)(2,1)} %get-tuple-element.15) | copy-start | bytes 196612
  196.0 21.6 %copy-start.23 = (bf16[64,8,8,8]{0,3,2,1:T(8,128)(2,1)S(1)}, bf16[64,8,8,8]{0,3,2,1:T(8,128)(2,1)}, u32[]{:S(2)}) copy-start(bf16[64,8,8,8]{0,3,2,1:T(8,128)(2,1)} %get-tuple-element.14) | copy-start | bytes 196612
  197.7 20.0 %copy-start.22 = (bf16[64,8,8,8]{0,3,2,1:T(8,128)(2,1)S(1)}, bf16[64,8,8,8]{0,3,2,1:T(8,128)(2,1)}, u32[]{:S(2)}) copy-start(bf16[64,8,8,8]{0,3,2,1:T(8,128)(2,1)} %get-tuple-element.13) | copy-start | bytes 196612
  217.7 19.6 %copy-start.82 = (bf16[1,64,512]{2,1,0:T(8,128)(2,1)S(1)}, bf16[1,64,512]{2,1,0:T(8,128)(2,1)}, u32[]{:S(2)}) copy-start(bf16[1,64,512]{2,1,0:T(8,128)(2,1)} %copy.317) | copy-start | bytes 196612
  217.7 19.6 %copy-start.80 = (bf16[1,64,512]{2,1,0:T(8,128)(2,1)S(1)}, bf16[1,64,512]{2,1,0:T(8,128)(2,1)}, u32[]{:S(2)}) copy-start(bf16[1,64,512]{2,1,0:T(8,128)(2,1)} %copy.318) | copy-start | bytes 196612
  217.9 19.5 %copy-start.78 = (bf16[1,64,512]{2,1,0:T(8,128)(2,1)S(1)}, bf16[1,64,512]{2,1,0:T(8,128)(2,1)}, u32[]{:S(2)}) copy-start(bf16[1,64,512]{2,1,0:T(8,128)(2,1)} %copy.319) | copy-start | bytes 196612
  218.0 19.4 %copy-start.75 = (bf16[1,64,512]{2,1,0:T(8,128)(2,1)S(1)}, bf16[1,64,512]{2,1,0:T(8,128)(2,1)}, u32[]{:S(2)}) copy-start(bf16[1,64,512]{2,1,0:T(8,128)(2,1)} %copy.320) | copy-start | bytes 196612
  218.0 19.4 %copy-start.71 = (bf16[1,64,512]{2,1,0:T(8,128)(2,1)S(1)}, bf16[1,64,512]{2,1,0:T(8,128)(2,1)}, u32[]{:S(2)}) copy-start(bf16[1,64,512]{2,1,0:T(8,128)(2,1)} %copy.321) | copy-start | bytes 196612
  (100 other events, 721.4 us)
Sparse Core Ops, SparseCore 0:
  158.4 104.8 all-gather.2
